TPU v7x, 128 devices: a whole 4x4x4 slice. The times are simulated.
128 devices in a mesh: row: 8 (over z, core), col: 16 (over x, y).
Axes of the slice: x: 4, y: 4, z: 4, core: 2. Of those that a mesh axis runs over, the one named last changes fastest.
Arguments:
- front_panel: float32 [40960, 512], P('row', 'col'), may hold values from -16 to 48, as said below
- front_slab: float32 [40960, 8192], P('row', 'col'), may hold values from -6 to 6
- child_one: bfloat16 [8192, 8192], P('col', 'row'), may hold values from -6 to 6
- child_two: bfloat16 [8192, 8192], P('col', 'row'), may hold values from -6 to 6
- map_one: int32 [32], replicated, may hold values from 0 to 159, as said below
- map_two: int32 [32], replicated, may hold values from 0 to 159, as said below
Outputs:
- factor_panel: float32 [40960, 512], P('row', 'col')
- slab_out: float32 [40960, 8192], P('row', 'col')
Inputs may be any that keep to these rules, and one draw needn't show every extreme that they name: `front_panel`: its first 512 rows are, in all 512 columns, a symmetric positive definite block. `map_one`: distinct root row blocks. Of the 20 blocks of one index of row (numbers k * 20 to (k + 1) * 20 - 1) at most 8 are named, and exactly 8 for some index of row. `map_two`: as map_one, drawn independently.
All inputs are finite; a program needn't handle non-finite values.
Results may differ from a plain program's by a relative error of at most 0.0003.
Values may be sent and summed in bfloat16 or wider, within the bound.
A program may use at most 192 MiB of HBM per device.

v0:
```python
import jax
import jax.numpy as jnp
from jax import lax
from jax.sharding import PartitionSpec as P

P_SIZE = 256
BLK = 256


def from_root(value, axis, source):
    kept = jnp.where(lax.axis_index(axis) == source, value, 0).astype(value.dtype)
    return lax.psum(kept, axis)


def inverse_factor(block):
    lower = jnp.linalg.cholesky(block)
    identity = jnp.eye(P_SIZE, dtype=jnp.float32)
    return jax.scipy.linalg.solve_triangular(lower, identity, lower=True)


def diagonal_work(top):
    highest = lax.Precision.HIGHEST
    inverse_one = inverse_factor(top[:P_SIZE, :P_SIZE])
    first_top = jnp.dot(
        top[P_SIZE:, :P_SIZE], inverse_one.T, precision=highest, preferred_element_type=jnp.float32
    )
    second_top = top[P_SIZE:, P_SIZE:] - jnp.dot(
        first_top, first_top.T, precision=highest, preferred_element_type=jnp.float32
    )
    inverse_two = inverse_factor(second_top)
    return (inverse_one, first_top, inverse_two)


def panel_rows(panel, inverse_one, first_top, inverse_two):
    highest = lax.Precision.HIGHEST
    first_cols = jnp.dot(
        panel[:, :P_SIZE], inverse_one.T, precision=highest, preferred_element_type=jnp.float32
    )
    second_in = panel[:, P_SIZE:] - jnp.dot(
        first_cols, first_top.T, precision=highest, preferred_element_type=jnp.float32
    )
    second_cols = jnp.dot(
        second_in, inverse_two.T, precision=highest, preferred_element_type=jnp.float32
    )
    return jnp.concatenate([first_cols, second_cols], 1)


def routing(mapping, local_blocks, row_count):
    owner = mapping // local_blocks
    owner_hot = (owner[:, None] == jnp.arange(row_count, dtype=jnp.int32)[None, :]).astype(
        jnp.int32
    )
    rank = jnp.sum(owner_hot * (jnp.cumsum(owner_hot, 0) - 1), 1)
    return (owner, rank, mapping % local_blocks)


def per_device(front_panel, front_slab, child_one, child_two, map_one, map_two):
    rows_dev = front_slab.shape[0]
    slab_width = front_slab.shape[1]
    panel_width = front_panel.shape[1]
    child_blocks = map_one.shape[0]
    child_local = child_one.shape[0]
    row_count = lax.axis_size("row")
    col_count = lax.axis_size("col")
    row_rank = lax.axis_index("row")
    col_rank = lax.axis_index("col")
    piece = slab_width // row_count
    local_blocks = rows_dev // BLK
    capacity = 2 * child_blocks // row_count

    def split_columns(child):
        return child.reshape(child_local, col_count, piece)

    got_one, got_two = (
        lax.all_to_all(split_columns(child_one), "col", split_axis=1, concat_axis=0, tiled=True),
        lax.all_to_all(split_columns(child_two), "col", split_axis=1, concat_axis=0, tiled=True),
    )

    def send_rows(received, mapping):
        owner, rank, target = routing(mapping, local_blocks, row_count)
        slot = owner * capacity + rank
        select = (
            slot[None, :] == jnp.arange(row_count * capacity, dtype=jnp.int32)[:, None]
        ).astype(jnp.bfloat16)
        blocks = received.reshape(child_blocks, BLK * piece)
        packed = jnp.dot(select, blocks, preferred_element_type=jnp.float32).astype(jnp.bfloat16)
        return packed.reshape(row_count * capacity * BLK, piece)

    arrived_one, arrived_two = (
        lax.all_to_all(send_rows(got_one, map_one), "row", split_axis=0, concat_axis=1, tiled=True),
        lax.all_to_all(send_rows(got_two, map_two), "row", split_axis=0, concat_axis=1, tiled=True),
    )

    def place(arrived, mapping):
        owner, rank, target = routing(mapping, local_blocks, row_count)
        mine = (owner == row_rank)[None, :, None]
        at_block = target[None, :, None] == jnp.arange(local_blocks, dtype=jnp.int32)[:, None, None]
        at_slot = rank[None, :, None] == jnp.arange(capacity, dtype=jnp.int32)[None, None, :]
        placing = jnp.sum((at_block & at_slot & mine).astype(jnp.int32), 1).astype(jnp.bfloat16)
        added = jnp.dot(
            placing, arrived.reshape(capacity, BLK * slab_width), preferred_element_type=jnp.float32
        )
        return added.reshape(rows_dev, slab_width)

    assembled = front_slab + place(arrived_one, map_one) + place(arrived_two, map_two)
    gathered = lax.all_gather(front_panel, "col", axis=1, tiled=True)
    top = gathered[: 2 * P_SIZE]
    top = from_root(top, "row", 0)
    inverse_one, first_top, inverse_two = diagonal_work(top)
    factor = panel_rows(gathered, inverse_one, first_top, inverse_two)
    factor_out = lax.dynamic_slice_in_dim(factor, col_rank * panel_width, panel_width, 1)
    global_rows = row_rank * rows_dev + jnp.arange(rows_dev, dtype=jnp.int32)
    masked = factor * (global_rows >= 2 * P_SIZE)[:, None].astype(jnp.float32)
    wanted = (
        2 * P_SIZE
        + col_rank * slab_width
        + jnp.arange(slab_width, dtype=jnp.int32)
        - row_rank * rows_dev
    )
    valid = ((wanted >= 0) & (wanted < rows_dev))[:, None].astype(jnp.float32)
    picked = jnp.take(factor, jnp.clip(wanted, 0, rows_dev - 1), axis=0) * valid
    slab_rows = lax.psum(picked, "row")
    update = jnp.dot(
        masked, slab_rows.T, precision=lax.Precision.HIGHEST, preferred_element_type=jnp.float32
    )
    return (factor_out, assembled - update)


def solution(mesh):
    in_specs = (P("row", "col"), P("row", "col"), P("col", "row"), P("col", "row"), P(), P())
    out_specs = (P("row", "col"), P("row", "col"))
    return jax.shard_map(
        per_device, mesh=mesh, in_specs=in_specs, out_specs=out_specs, check_vma=False
    )
```

profile of v0, /device:TPU:0, one launch (start us, length us, event | category | flops | bytes accessed | tf_op | source)
XLA Modules:
  0.0 495.1 jit_solution(5786572889173300262)
XLA Ops:
  7.2 0.7 all-gather.2.cloned.1.call-update
  7.9 2.3 copy.39
  10.2 7.1 %all-to-all-start = ((bf16[512,16,64]{0,2,1:T(8,128)(2,1)}), bf16[512,16,64]{0,2,1:T(8,128)(2,1)S(1)}, u32[]{:S(2)}, u32[]{:S(2)}) async-start(bf16[512,16,64]{0,2,1:T(8,128)(2,1)} %bitcast.11), calls=%async_computation | async-start | bytes 2097152 | tf_op jit(solution)/shard_map/all_to_all | solution.py:75
  17.4 1.3 copy.43
  18.7 19.1 %all-to-all-done = bf16[512,16,64]{0,2,1:T(8,128)(2,1)S(1)} async-done(((bf16[512,16,64]{0,2,1:T(8,128)(2,1)}), bf16[512,16,64]{0,2,1:T(8,128)(2,1)S(1)}, u32[]{:S(2)}, u32[]{:S(2)}) %all-to-all-start) | async-done | bytes 1048608 | tf_op jit(solution)/shard_map/all_to_all | solution.py:75
  37.8 6.6 %all-to-all-start.2 = ((bf16[512,16,64]{0,2,1:T(8,128)(2,1)}), bf16[512,16,64]{0,2,1:T(8,128)(2,1)S(1)}, u32[]{:S(2)}, u32[]{:S(2)}) async-start(bf16[512,16,64]{0,2,1:T(8,128)(2,1)} %bitcast.15), calls=%async_computation.2 | async-start | bytes 2097152 | tf_op jit(solution)/shard_map/all_to_all | solution.py:76
  44.8 2.0 copy.40
  46.8 2.5 reshape.193
  49.3 1.9 convolution_convert_fusion.1
  51.2 5.5 %all_to_all.49 = bf16[8,2048,64]{2,1,0:T(8,128)(2,1)} reshape(bf16[64,16384]{1,0:T(8,128)(2,1)S(1)} %convolution_convert_fusion.1) | data formatting | bytes 4194304 | tf_op jit(solution)/shard_map/all_to_all | solution.py:90
  56.7 4.8 copy.41
  61.5 6.5 %all-to-all-start.1 = ((bf16[8,2048,64]{1,2,0:T(8,128)(2,1)}), bf16[8,2048,64]{1,2,0:T(8,128)(2,1)S(1)}, u32[]{:S(2)}, u32[]{:S(2)}) async-start(bf16[8,2048,64]{1,2,0:T(8,128)(2,1)} %copy.41), calls=%async_computation.1 | async-start | bytes 4194304 | tf_op jit(solution)/shard_map/all_to_all | solution.py:90
  68.4 1.8 copy.44
  70.2 2.8 reshape.197
  73.1 2.0 convolution_convert_fusion
  75.1 6.5 %all_to_all.55 = bf16[8,2048,64]{2,1,0:T(8,128)(2,1)} reshape(bf16[64,16384]{1,0:T(8,128)(2,1)} %convolution_convert_fusion) | data formatting | bytes 4194304 | tf_op jit(solution)/shard_map/all_to_all | solution.py:91
  81.6 4.8 copy.45
  86.4 8.9 %all-to-all-done.1 = bf16[8,2048,64]{1,2,0:T(8,128)(2,1)S(1)} async-done(((bf16[8,2048,64]{1,2,0:T(8,128)(2,1)}), bf16[8,2048,64]{1,2,0:T(8,128)(2,1)S(1)}, u32[]{:S(2)}, u32[]{:S(2)}) %all-to-all-start.1) | async-done | bytes 2097184 | tf_op jit(solution)/shard_map/all_to_all | solution.py:90
  95.2 4.3 all-to-all-start.3
  100.8 4.2 copy.42
  105.0 5.0 %reshape.232 = bf16[1048576]{0:T(1024)(128)(2,1)S(1)} reshape(bf16[2048,8,64]{2,1,0:T(8,128)(2,1)} %copy.42) | data formatting | bytes 4194304
  110.1 2.2 reshape.194
  112.3 7.9 %fusion.38 = f32[20,131072]{1,0:T(8,128)} fusion(bf16[8,131072]{1,0:T(8,128)(2,1)} %reshape.194, s32[20,8]{1,0:T(8,128)S(1)} %convert_reduce_fusion.1), kind=kOutput, calls=%fused_computation.86 | convolution fusion | flops 41943200 | bytes 12583552 | tf_op jit(solution)/shard_map/dot_general | solution.py:100
  120.2 10.5 %reshape.195 = f32[5120,512]{1,0:T(8,128)} reshape(f32[20,131072]{1,0:T(8,128)} %fusion.38) | data formatting | bytes 20971520 | tf_op jit(solution)/shard_map/reshape | solution.py:103
  130.7 5.6 %copy.46 = bf16[2048,8,64]{2,1,0:T(8,128)(2,1)} copy(bf16[2048,8,64]{0,2,1:T(8,128)(2,1)} %bitcast.18) | data formatting | bytes 4194304 | tf_op jit(solution)/shard_map/all_to_all | solution.py:91
  136.4 5.0 %reshape.230 = bf16[1048576]{0:T(1024)(128)(2,1)S(1)} reshape(bf16[2048,8,64]{2,1,0:T(8,128)(2,1)} %copy.46) | data formatting | bytes 4194304
  141.4 2.2 reshape.198
  143.6 2.3 slice_select_fusion
  146.0 7.9 %fusion.36 = f32[20,131072]{1,0:T(8,128)} fusion(bf16[8,131072]{1,0:T(8,128)(2,1)} %reshape.198, s32[20,8]{1,0:T(8,128)S(1)} %convert_reduce_fusion), kind=kOutput, calls=%fused_computation.84 | convolution fusion | flops 41943200 | bytes 12583552 | tf_op jit(solution)/shard_map/dot_general | solution.py:100
  153.9 11.0 %reshape.199 = f32[5120,512]{1,0:T(8,128)} reshape(f32[20,131072]{1,0:T(8,128)} %fusion.36) | data formatting | bytes 20971520 | tf_op jit(solution)/shard_map/reshape | solution.py:103
  164.9 45.9 %all-reduce.4.cloned.1.call-done = f32[512,512]{0,1:T(8,128)} async-done(((f32[512,512]{0,1:T(8,128)}), f32[512,512]{0,1:T(8,128)}) %all-reduce.4.cloned.1.call-update) | async-done | bytes 1048592 | tf_op jit(solution)/shard_map/psum | solution.py:12
  210.9 1.1 slice.73
  212.1 1.0 fusion.15
  213.1 11.7 %cholesky.130 = f32[128,128]{1,0:T(8,128)S(1)} custom-call(f32[128,128]{1,0:T(8,128)S(1)} %cholesky.194), custom_call_target="Cholesky" | custom-call | tf_op jit(solution)/shard_map/jit(cholesky)/cholesky | solution.py:16
  224.8 9.8 %custom-call.13 = f32[1,128,128]{1,2,0:T(8,128)S(1)} custom-call(f32[1,128,128]{2,1,0:T(8,128)S(1)} %get-tuple-element.51), custom_call_target="InvertDiagBlocksLowerTriangular" | custom-call | tf_op jit(solution)/shard_map/jit(cholesky)/cholesky | solution.py:16
  235.1 11.7 %cholesky.147 = f32[128,128]{1,0:T(8,128)S(1)} custom-call(f32[128,128]{1,0:T(8,128)S(1)} %convolution_subtract_fusion.5), custom_call_target="Cholesky" | custom-call | tf_op jit(solution)/shard_map/jit(cholesky)/cholesky | solution.py:16
  246.9 0.7 compare_reduce_fusion.2
  248.9 3.9 while.4
  248.9 0.6 fusion.69
  249.5 1.3 bitcast_dynamic-update-slice_fusion.4
  250.9 0.6 fusion.69
  251.5 1.3 bitcast_dynamic-update-slice_fusion.4
  252.8 19.8 %custom-call.14 = f32[2,128,128]{1,2,0:T(8,128)S(1)} custom-call(f32[2,128,128]{2,1,0:T(8,128)S(1)} %get-tuple-element.18), custom_call_target="InvertDiagBlocksLowerTriangular" | custom-call | tf_op jit(solution)/shard_map/jit(_solve_triangular)/triangular_solve | solution.py:18
  273.6 0.6 fusion.8
  274.8 11.7 %cholesky.164 = f32[128,128]{1,0:T(8,128)S(1)} custom-call(f32[128,128]{1,0:T(8,128)S(1)} %cholesky.197), custom_call_target="Cholesky" | custom-call | tf_op jit(solution)/shard_map/jit(cholesky)/cholesky | solution.py:16
  286.5 9.8 %custom-call.15 = f32[1,128,128]{1,2,0:T(8,128)S(1)} custom-call(f32[1,128,128]{2,1,0:T(8,128)S(1)} %get-tuple-element.47), custom_call_target="InvertDiagBlocksLowerTriangular" | custom-call | tf_op jit(solution)/shard_map/jit(cholesky)/cholesky | solution.py:16
  296.8 11.7 %cholesky.181 = f32[128,128]{1,0:T(8,128)S(1)} custom-call(f32[128,128]{1,0:T(8,128)S(1)} %convolution_subtract_fusion.4), custom_call_target="Cholesky" | custom-call | tf_op jit(solution)/shard_map/jit(cholesky)/cholesky | solution.py:16
  308.6 0.7 compare_reduce_fusion
  309.3 0.6 compare_reduce_fusion.1
  311.3 4.1 while.5
  311.3 0.6 fusion.70
  311.9 1.4 bitcast_dynamic-update-slice_fusion.5
  313.9 1.4 bitcast_dynamic-update-slice_fusion.5
  315.4 19.9 %custom-call.16 = f32[2,128,128]{1,2,0:T(8,128)S(1)} custom-call(f32[2,128,128]{2,1,0:T(8,128)S(1)} %get-tuple-element.19), custom_call_target="InvertDiagBlocksLowerTriangular" | custom-call | tf_op jit(solution)/shard_map/jit(_solve_triangular)/triangular_solve | solution.py:18
  336.2 6.7 %fusion.4 = f32[256,5120]{1,0:T(8,128)S(1)} fusion(f32[5120,512]{0,1:T(8,128)} %all-gather.2.cloned.1.call-done, f32[128,256]{1,0:T(8,128)S(1)} %fusion.26, f32[128,256]{1,0:T(8,128)S(1)} %fusion.19), kind=kOutput, calls=%fused_computation.14 | convolution fusion | flops 4026597376 | bytes 10747904 | tf_op jit(solution)/shard_map/dot_general | solution.py:36
  342.9 9.0 %convolution_subtract_fusion = f32[5120,256]{0,1:T(8,128)S(1)} fusion(f32[256,5120]{1,0:T(8,128)S(1)} %fusion.4, f32[256,256]{1,0:T(8,128)S(1)} %fusion.8, f32[5120,512]{0,1:T(8,128)} %all-gather.2.cloned.1.call-done), kind=kOutput, calls=%fused_computation.13 | convolution fusion | flops 4027842560 | bytes 15990784 | tf_op jit(solution)/shard_map/dot_general | solution.py:39
  351.9 6.5 %fusion.10 = f32[5120,256]{0,1:T(8,128)} fusion(f32[5120,256]{0,1:T(8,128)S(1)} %convolution_subtract_fusion, f32[128,256]{1,0:T(8,128)S(1)} %fusion.22, f32[128,256]{1,0:T(8,128)S(1)} %fusion.17), kind=kOutput, calls=%fused_computation.30 | convolution fusion | flops 4026597376 | bytes 10747904 | tf_op jit(solution)/shard_map/dot_general | solution.py:42
  358.4 9.3 %pad_maximum_fusion = f32[5120,512]{0,1:T(8,128)} fusion(f32[5120,256]{0,1:T(8,128)} %fusion.10, f32[5120,256]{0,1:T(8,128)} %bitcast.92), kind=kLoop, calls=%fused_computation.8 | loop fusion | flops 2621440 | bytes 20971520 | tf_op jit(solution)/shard_map/concatenate | solution.py:45
  367.7 11.4 %copy.47 = f32[5120,512]{1,0:T(8,128)} copy(f32[5120,512]{0,1:T(8,128)} %pad_maximum_fusion) | data formatting | bytes 20971520 | tf_op jit(solution)/shard_map/concatenate | solution.py:45
  379.1 6.2 %gather_fusion = f32[512,512]{1,0:T(8,128)S(1)} fusion(f32[5120,512]{1,0:T(8,128)} %copy.47, s32[1024]{0:T(1024)S(1)} %pad_clamp_fusion), kind=kCustom, calls=%fused_computation | custom fusion | bytes 2099200 | tf_op jit(solution)/shard_map/jit(_take)/gather | solution.py:121
  385.4 1.2 select_multiply_fusion
  386.6 2.0 fusion.7
  388.6 60.0 %all-reduce.6.cloned.1.call-done = f32[512,512]{1,0:T(8,128)} async-done(((f32[512,512]{1,0:T(8,128)}), f32[512,512]{1,0:T(8,128)}) %all-reduce.6.cloned.1.call-update) | async-done | bytes 1048592 | tf_op jit(solution)/shard_map/psum | solution.py:122
  448.6 39.6 %add_subtract_fusion = f32[5120,512]{1,0:T(8,128)} fusion(f32[5120,512]{1,0:T(8,128)} %reshape.199, f32[5120,512]{1,0:T(8,128)} %param.10, f32[5120,512]{1,0:T(8,128)} %reshape.195, f32[512,512]{1,0:T(8,128)} %all-reduce.6.cloned.1.call-done, f32[5120]{0:T(1024)S(1)} %fusion.31, f32[5120,256]{0,1:T(8,128)} %fusion.10, f32[5120,256]{0,1:T(8,128)} %bitcast.94), kind=kOutput, calls=%fused_computation.12 | convolution fusion | flops 16119234560 | bytes 53497856 | tf_op jit(solution)/shard_map/dot_general | solution.py:123
  (74 shorter events, 6.3 us)
Async XLA Ops:
  7.2 10.2 %copy-start.3 = (bf16[512,1024]{1,0:T(8,128)(2,1)S(1)}, bf16[512,1024]{1,0:T(8,128)(2,1)}, u32[]{:S(2)}) copy-start(bf16[512,1024]{1,0:T(8,128)(2,1)} %param.12) | copy-start | bytes 3145732
  7.2 37.2 %copy-start.5 = (s32[32]{0:T(128)S(1)}, s32[32]{0:T(128)}, u32[]{:S(2)}) copy-start(s32[32]{0:T(128)} %param.13) | copy-start | bytes 388
  7.2 37.2 %copy-start.4 = (s32[32]{0:T(128)S(1)}, s32[32]{0:T(128)}, u32[]{:S(2)}) copy-start(s32[32]{0:T(128)} %param.14) | copy-start | bytes 388
  7.2 136.4 %all-gather.2.cloned.1.call-start = ((), (), s32[]{:S(2)}) async-start(), calls=%async_computation.4 | async-start | bytes 11141120 | tf_op jit(solution)/shard_map/all_gather | solution.py:106
  10.2 27.6 %all-to-all-start = ((bf16[512,16,64]{0,2,1:T(8,128)(2,1)}), bf16[512,16,64]{0,2,1:T(8,128)(2,1)S(1)}, u32[]{:S(2)}, u32[]{:S(2)}) async-start(bf16[512,16,64]{0,2,1:T(8,128)(2,1)} %bitcast.11), calls=%async_computation | async-start | bytes 2097152 | tf_op jit(solution)/shard_map/all_to_all | solution.py:75
  37.8 7.0 %copy-start.1 = (bf16[512,16,64]{0,2,1:T(8,128)(2,1)}, bf16[512,16,64]{0,2,1:T(8,128)(2,1)S(1)}, u32[]{:S(2)}) copy-start(bf16[512,16,64]{0,2,1:T(8,128)(2,1)S(1)} %all-to-all-done) | copy-start | bytes 3145732
  37.8 23.7 %all-to-all-start.2 = ((bf16[512,16,64]{0,2,1:T(8,128)(2,1)}), bf16[512,16,64]{0,2,1:T(8,128)(2,1)S(1)}, u32[]{:S(2)}, u32[]{:S(2)}) async-start(bf16[512,16,64]{0,2,1:T(8,128)(2,1)} %bitcast.15), calls=%async_computation.2 | async-start | bytes 2097152 | tf_op jit(solution)/shard_map/all_to_all | solution.py:76
  61.5 33.7 %all-to-all-start.1 = ((bf16[8,2048,64]{1,2,0:T(8,128)(2,1)}), bf16[8,2048,64]{1,2,0:T(8,128)(2,1)S(1)}, u32[]{:S(2)}, u32[]{:S(2)}) async-start(bf16[8,2048,64]{1,2,0:T(8,128)(2,1)} %copy.41), calls=%async_computation.1 | async-start | bytes 4194304 | tf_op jit(solution)/shard_map/all_to_all | solution.py:90
  95.2 35.5 %all-to-all-start.3 = ((bf16[8,2048,64]{1,2,0:T(8,128)(2,1)}), bf16[8,2048,64]{1,2,0:T(8,128)(2,1)}, u32[]{:S(2)}, u32[]{:S(2)}) async-start(bf16[8,2048,64]{1,2,0:T(8,128)(2,1)} %copy.45), calls=%async_computation.3 | async-start | bytes 4194304 | tf_op jit(solution)/shard_map/all_to_all | solution.py:91
  99.6 111.3 %all-reduce.4.cloned.1.call-start = ((), (), s32[]{:S(2)}) async-start(), calls=%async_computation.5 | async-start | bytes 2097152 | tf_op jit(solution)/shard_map/psum | solution.py:12
  146.0 302.6 %all-reduce.6.cloned.1.call-start = ((), (), s32[]{:S(2)}) async-start(), calls=%async_computation.6 | async-start | bytes 2097152 | tf_op jit(solution)/shard_map/psum | solution.py:122
  210.9 62.7 %copy-start.2 = (f32[512,512]{0,1:T(8,128)S(1)}, f32[512,512]{0,1:T(8,128)}, u32[]{:S(2)}) copy-start(f32[512,512]{0,1:T(8,128)} %all-reduce.4.cloned.1.call-done) | copy-start | bytes 3145732
  342.9 9.0 %copy-start = (f32[256,5120]{1,0:T(8,128)}, f32[256,5120]{1,0:T(8,128)S(1)}, u32[]{:S(2)}) copy-start(f32[256,5120]{1,0:T(8,128)S(1)} %fusion.4) | copy-start | bytes 15728644
Sparse Core Ops, SparseCore 0:
  10.2 89.2 all-gather.1
  146.1 64.7 all-reduce.3
  386.7 61.7 all-reduce.5
where the time goes:
time: 502 us; the launch traced here: 495 us
  waiting for transfers between devices  135 us (27%)
  other arithmetic  126 us (25%)
  local copies, waits for them, and re-layouts  107 us (21%)
  matrix products  85.3 us (17%)
  starting transfers between devices  24.9 us (5%)
  between operations  17.2 us (3%)
    another operation x13, other arithmetic, inverse_factor(): lower = jnp.linalg.cholesky(block)  68.6 us
    psum x1, waiting for transfers between devices, per_device(): slab_rows = lax.psum(picked, 'row')  60 us
    psum x1, waiting for transfers between devices, from_root(): return lax.psum(kept, axis)  45.9 us
    another operation x5, other arithmetic, inverse_factor(): return jax.scipy.linalg.solve_triangular(lower, identity, lower=True)  39.8 us
    dot_general x1, matrix products, per_device(): jnp.dot(masked, slab_rows.T, precision=lax.Precision.HIGHEST, preferred_e...  39.6 us
    reshape x2, local copies, waits for them, and re-layouts, place(): return added.reshape(rows_dev, slab_width)  21.5 us
    all_to_all x1, waiting for transfers between devices, per_device(): lax.all_to_all(split_columns(child_one), 'col', split_axis=1, concat_axis...  19.1 us
    all_to_all x3, local copies, waits for them, and re-layouts, per_device(): lax.all_to_all(send_rows(got_two, map_two), 'row', split_axis=0, concat_a...  16.9 us
  transfers between devices with their start and end apart: 7, of which 4 were waited for; matrix products, arithmetic and copies ran while one was open for 18% of the time, Pallas kernels for 0%

commit v1 on v0

--- a/solution.py
+++ b/solution.py
@@ -9,7 +9,7 @@
 
 def from_root(value, axis, source):
     kept = jnp.where(lax.axis_index(axis) == source, value, 0).astype(value.dtype)
-    return lax.psum(kept, axis)
+    return jnp.sum(lax.all_gather(kept, axis), axis=0)
 
 
 def inverse_factor(block):

time: 502 us -> 558 us (1.11)
  waiting for transfers between devices: 135 us -> 173 us
  local copies, waits for them, and re-layouts: 107 us -> 127 us
  starting transfers between devices: 24.9 us -> 17.9 us
    all_gather x1, waiting for transfers between devices: 0.01 us -> 85 us  [per_device(): gathered = lax.all_gather(front_panel, 'col', axis=1, tiled=True)]
    psum x1 -> x0, waiting for transfers between devices: 45.9 us -> none  [from_root(): return lax.psum(kept, axis)]
    all_gather x0 -> x1, local copies, waits for them, and re-layouts: none -> 9 us  [from_root(): return jnp.sum(lax.all_gather(kept, axis), axis=0)]
    unnamed x16 -> x21, local copies, waits for them, and re-layouts: 13.7 us -> 20.1 us
  transfers between devices with their start and end apart: 7 -> 7, of which waited for: 4 -> 4; matrix products, arithmetic and copies ran while one was open for 18% -> 19% of each run, Pallas kernels for 0% -> 0%
where the time goes in v1:
time: 558 us; the launch traced here: 550 us
  waiting for transfers between devices  173 us (31%)
  other arithmetic  130 us (23%)
  local copies, waits for them, and re-layouts  127 us (23%)
  matrix products  85.3 us (15%)
  starting transfers between devices  17.9 us (3%)
  between operations  17 us (3%)
    all_gather x1, waiting for transfers between devices, per_device(): gathered = lax.all_gather(front_panel, 'col', axis=1, tiled=True)  85 us
    another operation x13, other arithmetic, inverse_factor(): lower = jnp.linalg.cholesky(block)  68.7 us
    psum x1, waiting for transfers between devices, per_device(): slab_rows = lax.psum(picked, 'row')  62.6 us
    another operation x5, other arithmetic, inverse_factor(): return jax.scipy.linalg.solve_triangular(lower, identity, lower=True)  40 us
    dot_general x1, matrix products, per_device(): jnp.dot(masked, slab_rows.T, precision=lax.Precision.HIGHEST, preferred_e...  39.6 us
    reshape x2, local copies, waits for them, and re-layouts, place(): return added.reshape(rows_dev, slab_width)  21.1 us
    unnamed x21, local copies, waits for them, and re-layouts  20.1 us
    all_to_all x3, local copies, waits for them, and re-layouts, per_device(): lax.all_to_all(send_rows(got_two, map_two), 'row', split_axis=0, concat_a...  16.9 us
  transfers between devices with their start and end apart: 7, of which 4 were waited for; matrix products, arithmetic and copies ran while one was open for 19% of the time, Pallas kernels for 0%

profile of v1, /device:TPU:0, one launch (start us, length us, event | category | flops | bytes accessed | tf_op | source)
XLA Modules:
  0.0 550.3 jit_solution(14118535015445356019)
XLA Ops:
  7.2 0.7 all-gather.4.cloned.1.call-update
  8.0 85.0 %all-gather.4.cloned.1.call-done = f32[5120,512]{0,1:T(8,128)} async-done(((f32[5120,32]{0,1:T(8,128)}), f32[5120,512]{0,1:T(8,128)}) %all-gather.4.cloned.1.call-update) | async-done | bytes 10485776 | tf_op jit(solution)/shard_map/all_gather | solution.py:106
  93.0 2.3 slice_select_fusion
  95.3 2.3 copy.58
  97.6 5.3 all-to-all-start
  102.9 1.3 copy.62
  104.2 16.4 %all-to-all-done = bf16[512,16,64]{0,2,1:T(8,128)(2,1)S(1)} async-done(((bf16[512,16,64]{0,2,1:T(8,128)(2,1)}), bf16[512,16,64]{0,2,1:T(8,128)(2,1)S(1)}, u32[]{:S(2)}, u32[]{:S(2)}) %all-to-all-start) | async-done | bytes 1048608 | tf_op jit(solution)/shard_map/all_to_all | solution.py:75
  120.6 3.7 all-to-all-start.2
  124.6 2.0 copy.59
  126.6 2.5 reshape.193
  129.1 1.9 convolution_convert_fusion.1
  131.0 5.5 %all_to_all.49 = bf16[8,2048,64]{2,1,0:T(8,128)(2,1)} reshape(bf16[64,16384]{1,0:T(8,128)(2,1)S(1)} %convolution_convert_fusion.1) | data formatting | bytes 4194304 | tf_op jit(solution)/shard_map/all_to_all | solution.py:90
  136.6 4.8 copy.60
  141.4 4.5 all-to-all-start.1
  146.2 1.8 copy.63
  148.0 2.8 reshape.197
  150.9 2.1 convolution_convert_fusion
  152.9 6.5 %all_to_all.55 = bf16[8,2048,64]{2,1,0:T(8,128)(2,1)} reshape(bf16[64,16384]{1,0:T(8,128)(2,1)} %convolution_convert_fusion) | data formatting | bytes 4194304 | tf_op jit(solution)/shard_map/all_to_all | solution.py:91
  159.4 4.8 copy.64
  164.2 8.8 %all-to-all-done.1 = bf16[8,2048,64]{1,2,0:T(8,128)(2,1)S(1)} async-done(((bf16[8,2048,64]{1,2,0:T(8,128)(2,1)}), bf16[8,2048,64]{1,2,0:T(8,128)(2,1)S(1)}, u32[]{:S(2)}, u32[]{:S(2)}) %all-to-all-start.1) | async-done | bytes 2097184 | tf_op jit(solution)/shard_map/all_to_all | solution.py:90
  173.0 4.4 all-to-all-start.3
  178.4 4.7 copy.61
  183.1 5.0 reshape.233
  188.1 2.2 reshape.194
  190.3 7.9 %fusion.38 = f32[20,131072]{1,0:T(8,128)} fusion(bf16[8,131072]{1,0:T(8,128)(2,1)} %reshape.194, s32[20,8]{1,0:T(8,128)S(1)} %convert_reduce_fusion.1), kind=kOutput, calls=%fused_computation.86 | convolution fusion | flops 41943200 | bytes 12583552 | tf_op jit(solution)/shard_map/dot_general | solution.py:100
  198.2 10.5 %reshape.195 = f32[5120,512]{1,0:T(8,128)} reshape(f32[20,131072]{1,0:T(8,128)} %fusion.38) | data formatting | bytes 20971520 | tf_op jit(solution)/shard_map/reshape | solution.py:103
  208.8 5.6 %copy.65 = bf16[2048,8,64]{2,1,0:T(8,128)(2,1)} copy(bf16[2048,8,64]{0,2,1:T(8,128)(2,1)} %bitcast.19) | data formatting | bytes 4194304 | tf_op jit(solution)/shard_map/all_to_all | solution.py:91
  214.4 5.0 reshape.231
  219.5 2.2 reshape.198
  221.7 7.9 %fusion.36 = f32[20,131072]{1,0:T(8,128)} fusion(bf16[8,131072]{1,0:T(8,128)(2,1)} %reshape.198, s32[20,8]{1,0:T(8,128)S(1)} %convert_reduce_fusion), kind=kOutput, calls=%fused_computation.84 | convolution fusion | flops 41943200 | bytes 12583552 | tf_op jit(solution)/shard_map/dot_general | solution.py:100
  229.6 10.5 %reshape.199 = f32[5120,512]{1,0:T(8,128)} reshape(f32[20,131072]{1,0:T(8,128)} %fusion.36) | data formatting | bytes 20971520 | tf_op jit(solution)/shard_map/reshape | solution.py:103
  240.1 5.4 slice.75
  245.5 6.1 %copy.70 = f32[5120,256]{1,0:T(8,128)} copy(f32[5120,256]{0,1:T(8,128)} %slice.75) | data formatting | bytes 10485760
  251.6 9.0 %copy.68 = f32[4096,512]{1,0:T(8,128)} copy(f32[4096,512]{0,1:T(8,128)} %all-gather.6.cloned.1.call-done) | data formatting | bytes 16777216 | tf_op jit(solution)/shard_map/all_gather | solution.py:12
  260.6 4.5 reduce_sum.43
  265.3 11.7 %cholesky.130 = f32[128,128]{1,0:T(8,128)S(1)} custom-call(f32[128,128]{1,0:T(8,128)S(1)} %cholesky.194), custom_call_target="Cholesky" | custom-call | tf_op jit(solution)/shard_map/jit(cholesky)/cholesky | solution.py:16
  277.1 9.8 %custom-call.13 = f32[1,128,128]{1,2,0:T(8,128)S(1)} custom-call(f32[1,128,128]{2,1,0:T(8,128)S(1)} %get-tuple-element.53), custom_call_target="InvertDiagBlocksLowerTriangular" | custom-call | tf_op jit(solution)/shard_map/jit(cholesky)/cholesky | solution.py:16
  287.4 11.7 %cholesky.147 = f32[128,128]{1,0:T(8,128)S(1)} custom-call(f32[128,128]{1,0:T(8,128)S(1)} %convolution_subtract_fusion.5), custom_call_target="Cholesky" | custom-call | tf_op jit(solution)/shard_map/jit(cholesky)/cholesky | solution.py:16
  299.2 0.7 compare_reduce_fusion.2
  301.2 4.1 while.4
  301.3 0.6 fusion.70
  301.9 1.3 bitcast_dynamic-update-slice_fusion.4
  303.3 0.6 fusion.70
  304.0 1.3 bitcast_dynamic-update-slice_fusion.4
  305.3 20.1 %custom-call.14 = f32[2,128,128]{1,2,0:T(8,128)S(1)} custom-call(f32[2,128,128]{2,1,0:T(8,128)S(1)} %get-tuple-element.18), custom_call_target="InvertDiagBlocksLowerTriangular" | custom-call | tf_op jit(solution)/shard_map/jit(_solve_triangular)/triangular_solve | solution.py:18
  327.5 11.7 %cholesky.164 = f32[128,128]{1,0:T(8,128)S(1)} custom-call(f32[128,128]{1,0:T(8,128)S(1)} %cholesky.197), custom_call_target="Cholesky" | custom-call | tf_op jit(solution)/shard_map/jit(cholesky)/cholesky | solution.py:16
  339.2 9.8 %custom-call.15 = f32[1,128,128]{1,2,0:T(8,128)S(1)} custom-call(f32[1,128,128]{2,1,0:T(8,128)S(1)} %get-tuple-element.49), custom_call_target="InvertDiagBlocksLowerTriangular" | custom-call | tf_op jit(solution)/shard_map/jit(cholesky)/cholesky | solution.py:16
  349.5 11.7 %cholesky.181 = f32[128,128]{1,0:T(8,128)S(1)} custom-call(f32[128,128]{1,0:T(8,128)S(1)} %convolution_subtract_fusion.4), custom_call_target="Cholesky" | custom-call | tf_op jit(solution)/shard_map/jit(cholesky)/cholesky | solution.py:16
  361.3 0.7 compare_reduce_fusion
  362.0 0.6 compare_reduce_fusion.1
  364.0 4.0 while.5
  364.6 1.4 bitcast_dynamic-update-slice_fusion.5
  366.6 1.4 bitcast_dynamic-update-slice_fusion.5
  367.9 19.8 %custom-call.16 = f32[2,128,128]{1,2,0:T(8,128)S(1)} custom-call(f32[2,128,128]{2,1,0:T(8,128)S(1)} %get-tuple-element.19), custom_call_target="InvertDiagBlocksLowerTriangular" | custom-call | tf_op jit(solution)/shard_map/jit(_solve_triangular)/triangular_solve | solution.py:18
  388.7 7.0 %fusion.4 = f32[256,5120]{1,0:T(8,128)S(1)} fusion(f32[5120,512]{0,1:T(8,128)} %all-gather.4.cloned.1.call-done, f32[128,256]{1,0:T(8,128)S(1)} %fusion.26, f32[128,256]{1,0:T(8,128)S(1)} %fusion.19), kind=kOutput, calls=%fused_computation.14 | convolution fusion | flops 4026597376 | bytes 10747904 | tf_op jit(solution)/shard_map/dot_general | solution.py:36
  395.7 8.9 %convolution_subtract_fusion = f32[5120,256]{1,0:T(8,128)S(1)} fusion(f32[5120,256]{1,0:T(8,128)S(1)} %bitcast.98, f32[256,5120]{1,0:T(8,128)S(1)} %fusion.4, f32[256,256]{1,0:T(8,128)S(1)} %fusion.8), kind=kOutput, calls=%fused_computation.13 | convolution fusion | flops 4027842560 | bytes 15990784 | tf_op jit(solution)/shard_map/dot_general | solution.py:39
  404.6 6.5 %fusion.10 = f32[5120,256]{0,1:T(8,128)} fusion(f32[5120,256]{1,0:T(8,128)S(1)} %convolution_subtract_fusion, f32[128,256]{1,0:T(8,128)S(1)} %fusion.22, f32[128,256]{1,0:T(8,128)S(1)} %fusion.17), kind=kOutput, calls=%fused_computation.30 | convolution fusion | flops 4026597376 | bytes 10747904 | tf_op jit(solution)/shard_map/dot_general | solution.py:42
  411.1 9.3 %pad_maximum_fusion = f32[5120,512]{0,1:T(8,128)} fusion(f32[5120,256]{0,1:T(8,128)} %fusion.10, f32[5120,256]{0,1:T(8,128)} %bitcast.93), kind=kLoop, calls=%fused_computation.8 | loop fusion | flops 2621440 | bytes 20971520 | tf_op jit(solution)/shard_map/concatenate | solution.py:45
  420.4 11.4 %copy.66 = f32[5120,512]{1,0:T(8,128)} copy(f32[5120,512]{0,1:T(8,128)} %pad_maximum_fusion) | data formatting | bytes 20971520 | tf_op jit(solution)/shard_map/concatenate | solution.py:45
  431.8 6.2 %gather_fusion = f32[512,512]{1,0:T(8,128)S(1)} fusion(f32[5120,512]{1,0:T(8,128)} %copy.66, s32[1024]{0:T(1024)S(1)} %pad_clamp_fusion), kind=kCustom, calls=%fused_computation | custom fusion | bytes 2099200 | tf_op jit(solution)/shard_map/jit(_take)/gather | solution.py:121
  438.0 1.2 select_multiply_fusion
  439.3 2.0 fusion.7
  441.3 62.6 %all-reduce.3.cloned.1.call-done = f32[512,512]{1,0:T(8,128)} async-done(((f32[512,512]{1,0:T(8,128)}), f32[512,512]{1,0:T(8,128)}) %all-reduce.3.cloned.1.call-update) | async-done | bytes 1048592 | tf_op jit(solution)/shard_map/psum | solution.py:122
  503.9 39.6 %add_subtract_fusion = f32[5120,512]{1,0:T(8,128)} fusion(f32[5120,512]{1,0:T(8,128)} %reshape.199, f32[5120,512]{1,0:T(8,128)} %param.10, f32[5120,512]{1,0:T(8,128)} %reshape.195, f32[512,512]{1,0:T(8,128)} %all-reduce.3.cloned.1.call-done, f32[5120]{0:T(1024)S(1)} %fusion.31, f32[5120,256]{0,1:T(8,128)} %fusion.10, f32[5120,256]{0,1:T(8,128)} %bitcast.95), kind=kOutput, calls=%fused_computation.12 | convolution fusion | flops 16119234560 | bytes 53497856 | tf_op jit(solution)/shard_map/dot_general | solution.py:123
  (82 shorter events, 7.3 us)
Async XLA Ops:
  7.2 95.7 %copy-start.2 = (bf16[512,1024]{1,0:T(8,128)(2,1)S(1)}, bf16[512,1024]{1,0:T(8,128)(2,1)}, u32[]{:S(2)}) copy-start(bf16[512,1024]{1,0:T(8,128)(2,1)} %param.12) | copy-start | bytes 3145732
  7.2 85.8 %all-gather.4.cloned.1.call-start = ((), (), s32[]{:S(2)}) async-start(), calls=%async_computation.4 | async-start | bytes 11141120 | tf_op jit(solution)/shard_map/all_gather | solution.py:106
  7.9 243.7 %all-gather.6.cloned.1.call-start = ((), (), s32[]{:S(2)}) async-start(), calls=%async_computation.6 | async-start | bytes 9437184 | tf_op jit(solution)/shard_map/all_gather | solution.py:12
  95.3 28.9 %copy-start.3 = (s32[32]{0:T(128)S(1)}, s32[32]{0:T(128)}, u32[]{:S(2)}) copy-start(s32[32]{0:T(128)} %param.14) | copy-start | bytes 388
  95.3 28.9 %copy-start.4 = (s32[32]{0:T(128)S(1)}, s32[32]{0:T(128)}, u32[]{:S(2)}) copy-start(s32[32]{0:T(128)} %param.13) | copy-start | bytes 388
  97.6 23.0 %all-to-all-start = ((bf16[512,16,64]{0,2,1:T(8,128)(2,1)}), bf16[512,16,64]{0,2,1:T(8,128)(2,1)S(1)}, u32[]{:S(2)}, u32[]{:S(2)}) async-start(bf16[512,16,64]{0,2,1:T(8,128)(2,1)} %bitcast.12), calls=%async_computation | async-start | bytes 2097152 | tf_op jit(solution)/shard_map/all_to_all | solution.py:75
  120.6 4.0 copy-start.1
  120.6 20.8 %all-to-all-start.2 = ((bf16[512,16,64]{0,2,1:T(8,128)(2,1)}), bf16[512,16,64]{0,2,1:T(8,128)(2,1)S(1)}, u32[]{:S(2)}, u32[]{:S(2)}) async-start(bf16[512,16,64]{0,2,1:T(8,128)(2,1)} %bitcast.16), calls=%async_computation.2 | async-start | bytes 2097152 | tf_op jit(solution)/shard_map/all_to_all | solution.py:76
  141.4 31.7 %all-to-all-start.1 = ((bf16[8,2048,64]{1,2,0:T(8,128)(2,1)}), bf16[8,2048,64]{1,2,0:T(8,128)(2,1)S(1)}, u32[]{:S(2)}, u32[]{:S(2)}) async-start(bf16[8,2048,64]{1,2,0:T(8,128)(2,1)} %copy.60), calls=%async_computation.1 | async-start | bytes 4194304 | tf_op jit(solution)/shard_map/all_to_all | solution.py:90
  173.0 35.7 %all-to-all-start.3 = ((bf16[8,2048,64]{1,2,0:T(8,128)(2,1)}), bf16[8,2048,64]{1,2,0:T(8,128)(2,1)}, u32[]{:S(2)}, u32[]{:S(2)}) async-start(bf16[8,2048,64]{1,2,0:T(8,128)(2,1)} %copy.64), calls=%async_computation.3 | async-start | bytes 4194304 | tf_op jit(solution)/shard_map/all_to_all | solution.py:91
  177.4 326.5 %all-reduce.3.cloned.1.call-start = ((), (), s32[]{:S(2)}) async-start(), calls=%async_computation.5 | async-start | bytes 2097152 | tf_op jit(solution)/shard_map/psum | solution.py:122
  388.1 7.6 %slice-start = ((s8[5242880]{0:T(1024)(128)(4,1)}), s8[4194304]{0:T(1024)(128)(4,1)S(1)}, s32[]{:S(2)}) async-start(s8[5242880]{0:T(1024)(128)(4,1)} %bitcast.97), calls=%async_computation.7 | async-start | bytes 8388608
  388.7 7.0 %slice-start.1 = ((s8[5242880]{0:T(1024)(128)(4,1)}), s8[1048576]{0:T(1024)(128)(4,1)S(1)}, s32[]{:S(2)}) async-start(s8[5242880]{0:T(1024)(128)(4,1)} %bitcast.97), calls=%async_computation.8 | async-start | bytes 2097152
  395.7 8.9 %copy-start = (f32[256,5120]{1,0:T(8,128)}, f32[256,5120]{1,0:T(8,128)S(1)}, u32[]{:S(2)}) copy-start(f32[256,5120]{1,0:T(8,128)S(1)} %fusion.4) | copy-start | bytes 15728644
Sparse Core Ops, SparseCore 0:
  10.2 82.7 all-gather.3
  95.4 49.5 all-gather.5
  439.4 64.4 all-reduce.2
